TPU v7x, 32 devices: a whole 2x2x4 slice. The times are simulated.
32 devices in a mesh: tile: 8 (over z, y), rcpt: 4 (over x, core).
Axes of the slice: x: 2, y: 2, z: 4, core: 2. Of those that a mesh axis runs over, the one named last changes fastest.
Arguments:
- adjoint_state: float32 [64, 16, 128, 256], P('rcpt', None, 'tile'), may hold values from -6 to 6
- met_fields: bfloat16 [12, 3, 16, 128, 256], P(None, None, 'rcpt', 'tile'), may hold values from -0.34960938 to 0.34960938
- forcing: bfloat16 [64, 128, 256], P(None, 'tile'), may hold values from -6 to 6
- cluster_ids: int32 [64], P('rcpt'), may hold values from 0 to 63
- hour_index: int32 [2], replicated, may hold values from 0 to 11
Outputs:
- adjoint_out: float32 [64, 16, 128, 256], P('rcpt', None, 'tile')
All inputs are finite; a program needn't handle non-finite values.
Results may differ from a plain program's by a relative error of at most 0.00035.
Values may be sent and summed in bfloat16 or wider, within the bound.
A program may use at most 64 MiB of HBM per device.

v0:
```python
import jax
import jax.numpy as jnp
from jax import lax
from jax.sharding import PartitionSpec as P

STEPS = 2


def for_sending(x):

    def short(part):
        return part.astype(jnp.bfloat16) if part.dtype == jnp.float32 else part

    return jax.tree.map(short, x)


def passed_along(block, axis, distance):
    devices = range(lax.axis_size(axis))
    route = [((i - distance) % len(devices), i) for i in devices]
    return lax.ppermute(block, axis, route)


def interior(lam, winds, east, west):
    cx = winds[0].astype(jnp.float32)
    cy = winds[1].astype(jnp.float32)
    py = lam * jnp.maximum(cy, 0.0)
    my = lam * jnp.minimum(cy, 0.0)
    zero = jnp.zeros_like(py[..., :1])
    north = jnp.concatenate([py[..., 1:], zero], axis=3)
    south = jnp.concatenate([zero, my[..., :-1]], axis=3)
    return lam * (1.0 - jnp.abs(cx) - jnp.abs(cy)) + east - west + north - south


def horizontal_shift(lam, winds):
    cx = winds[0].astype(jnp.float32)
    px = lam * jnp.maximum(cx, 0.0)
    mx = lam * jnp.minimum(cx, 0.0)
    east_edge = passed_along(for_sending(px[:, :, :1]), "tile", -1)
    west_edge = passed_along(for_sending(mx[:, :, -1:]), "tile", 1)
    east = jnp.concatenate([px[:, :, 1:], east_edge], axis=2)
    west = jnp.concatenate([west_edge, mx[:, :, :-1]], axis=2)
    return interior(lam, winds, east, west)


def vertical(lam, mixing):
    coeff = 0.02 + 0.25 * jnp.abs(mixing.astype(jnp.float32))
    flux = coeff[:-1] * (lam[:, 1:] - lam[:, :-1])
    zero = jnp.zeros_like(flux[:, :1])
    return jnp.concatenate([flux, zero], axis=1) - jnp.concatenate([zero, flux], axis=1)


def finish(lam, flat, mixing, source_rows):
    state = flat + vertical(lam, mixing)
    return state.at[:, -1].add(source_rows)


def per_device(adjoint_state, met_fields, forcing, cluster_ids, hour_index):
    lam = adjoint_state
    clusters = forcing.shape[0]
    onehot = (cluster_ids[:, None] == jnp.arange(clusters, dtype=jnp.int32)[None, :]).astype(
        jnp.bfloat16
    )
    source_rows = jnp.dot(onehot, forcing.reshape(clusters, -1), preferred_element_type=jnp.float32)
    source_rows = source_rows.reshape(lam.shape[0], lam.shape[2], lam.shape[3])
    locals_list = [
        lax.dynamic_index_in_dim(met_fields, hour_index[step], 0, keepdims=False)
        for step in range(STEPS)
    ]
    for step in range(STEPS):
        metnow = lax.all_gather(locals_list[step], "rcpt", axis=1, tiled=True)
        lam_next = finish(lam, horizontal_shift(lam, metnow), metnow[2], source_rows)
        lam = lam_next
    return lam


def solution(mesh):
    placed = (
        P("rcpt", None, "tile", None),
        P(None, None, "rcpt", "tile", None),
        P(None, "tile", None),
        P("rcpt"),
        P(),
    )
    return jax.shard_map(
        per_device,
        mesh=mesh,
        in_specs=placed,
        out_specs=P("rcpt", None, "tile", None),
        check_vma=False,
    )
```

profile of v0, /device:TPU:0, one launch (start us, length us, event | category | flops | bytes accessed | tf_op | source)
XLA Modules:
  0.0 91.9 jit_solution(882983224714222362)
XLA Ops:
  0.0 1.3 %fusion.32 = (s32[1]{0:T(128)}, s32[1]{0:T(128)}) fusion(s32[2]{0:T(128)} %param.13), kind=kLoop, calls=%fused_computation.69 | loop fusion | bytes 16 | tf_op jit(solution)/shard_map/slice | solution.py:66
  4.9 1.0 %constant_dynamic-slice_fusion = (bf16[1,3,4,16,256]{4,3,2,1,0:T(8,128)(2,1)S(1)}, bf16[1,3,4,16,256]{4,3,2,1,0:T(8,128)(2,1)S(1)}) fusion(bf16[12,3,4,16,256]{4,3,2,1,0:T(8,128)(2,1)} %param.10, s32[]{:T(128)S(6)} %select_n.8, s32[]{:T(128)S(6)} %select_n.7), kind=kLoop, calls=%fused_computation.66 | loop fusion | bytes 393224 | tf_op jit(solution)/shard_map/jit(dynamic_index_in_dim)/dynamic_slice | solution.py:66
  5.9 7.9 %all-gather = bf16[1,3,16,16,256]{4,3,2,1,0:T(8,128)(2,1)S(1)} all-gather(bf16[1,3,4,16,256]{4,3,2,1,0:T(8,128)(2,1)S(1)} %get-tuple-element.39), channel_id=2, replica_groups=mesh['tile'=8,'rcpt'=4] {'rcpt'}, dimensions={2}, use_global_device_ids=true | all-gather | bytes 491520 | tf_op jit(solution)/shard_map/all_gather | solution.py:70
  14.0 6.5 %fusion.31 = (f32[16,16,16,256]{3,0,2,1:T(8,128)S(1)}, f32[16,16,16,256]{3,0,2,1:T(8,128)S(1)}, f32[16,16,16,256]{3,0,2,1:T(8,128)S(1)}) fusion(f32[16,16,16,256]{3,2,1,0:T(8,128)} %param.9, f32[16,16,256]{2,1,0:T(8,128)S(1)} %get-tuple-element.47, f32[16,16,256]{2,1,0:T(8,128)S(1)} %get-tuple-element.50), kind=kLoop, calls=%fused_computation.68 | loop fusion | flops 2097152 | bytes 17301504 | tf_op args[0]
  20.6 0.7 slice.250
  21.2 1.5 %collective-permute-start.1 = (bf16[16,16,1,256]{3,0,2,1:T(8,128)(2,1)}, bf16[16,16,1,256]{3,0,2,1:T(8,128)(2,1)}, u32[]{:S(2)}, u32[]{:S(2)}) collective-permute-start(bf16[16,16,1,256]{3,0,2,1:T(8,128)(2,1)} %slice.250), channel_id=1, source_target_pairs={{28,0},{0,4},{4,8},{8,12},{12,16},{16,20},{20,24},{24,28},{29,1},{... | collective-permute-start | bytes 393224 | tf_op jit(solution)/shard_map/ppermute | solution.py:20
  22.7 0.7 slice.251
  23.4 3.2 %collective-permute-start = (bf16[16,16,1,256]{3,0,2,1:T(8,128)(2,1)}, bf16[16,16,1,256]{3,0,2,1:T(8,128)(2,1)}, u32[]{:S(2)}, u32[]{:S(2)}) collective-permute-start(bf16[16,16,1,256]{3,0,2,1:T(8,128)(2,1)} %slice.251), channel_id=1, source_target_pairs={{4,0},{8,4},{12,8},{16,12},{20,16},{24,20},{28,24},{0,28},{5,1},{9... | collective-permute-start | bytes 393224 | tf_op jit(solution)/shard_map/ppermute | solution.py:20
  26.6 2.3 %slice.182 = f32[16,16,15,256]{3,0,2,1:T(8,128)} slice(f32[16,16,16,256]{3,0,2,1:T(8,128)S(1)} %get-tuple-element.36), slice={[0:16], [0:16], [1:16], [0:256]} | slice | bytes 7864320 | tf_op jit(solution)/shard_map/slice | solution.py:40
  29.0 2.3 %slice.185 = f32[16,16,15,256]{3,0,2,1:T(8,128)} slice(f32[16,16,16,256]{3,0,2,1:T(8,128)S(1)} %get-tuple-element.37), slice={[0:16], [0:16], [0:15], [0:256]} | slice | bytes 7864320 | tf_op jit(solution)/shard_map/slice | solution.py:41
  31.3 6.3 %all-gather.1 = bf16[1,3,16,16,256]{4,3,2,1,0:T(8,128)(2,1)S(1)} all-gather(bf16[1,3,4,16,256]{4,3,2,1,0:T(8,128)(2,1)S(1)} %get-tuple-element.38), channel_id=3, replica_groups=mesh['tile'=8,'rcpt'=4] {'rcpt'}, dimensions={2}, use_global_device_ids=true | all-gather | bytes 491520 | tf_op jit(solution)/shard_map/all_gather | solution.py:70
  37.6 0.8 slice.187
  38.4 1.0 %fusion.22 = (f32[16,16,256]{2,1,0:T(8,128)S(1)}, f32[16,16,256]{2,1,0:T(8,128)}, f32[16,16,256]{2,1,0:T(8,128)S(1)}, f32[16,16,256]{2,1,0:T(8,128)S(1)}, f32[16,16,256]{2,1,0:T(8,128)}, /*index=5*/f32[1,16,16,256]{3,2,1,0:T(8,128)}) fusion(bf16[1,3,16,16,256]{4,3,2,1,0:T(8,128)(2,1)S(1)} %all-gather.1), kind=kLoop, calls=%fused_computation.47 | loop fusion | flops 917504 | bytes 1966080 | tf_op jit(solution)/shard_map/mul | solution.py:31
  39.4 0.9 slice.202
  40.3 2.5 %fusion.9 = f32[16,15,16,256]{3,0,2,1:T(8,128)} fusion(f32[16,16,16,256]{3,0,2,1:T(8,128)S(1)} %get-tuple-element.35, f32[15,16,256]{2,1,0:T(8,128)S(1)} %slice_bitcast_fusion.1), kind=kLoop, calls=%fused_computation.17 | loop fusion | flops 1966080 | bytes 12042240 | tf_op jit(solution)/shard_map/mul | solution.py:47
  42.8 3.0 %slice_multiply_fusion.3 = (f32[16,16,16,255]{3,0,2,1:T(8,128)S(1)}, f32[16,16,16,255]{3,0,2,1:T(8,128)S(1)}) fusion(f32[16,16,16,256]{3,0,2,1:T(8,128)S(1)} %get-tuple-element.35, f32[16,16,255]{2,1,0:T(8,128)} %slice.187, f32[16,16,255]{2,1,0:T(8,128)S(1)} %bitcast.53), kind=kLoop, calls=%fused_computation.3 | loop fusion | flops 2088960 | bytes 17233920 | tf_op jit(solution)/shard_map/mul | solution.py:26
  45.8 1.7 %slice_bitcast_fusion = f32[15,16,256]{2,1,0:T(8,128)} fusion(f32[1,16,16,256]{3,2,1,0:T(8,128)} %get-tuple-element.45), kind=kLoop, calls=%fused_computation.61 | loop fusion | bytes 491520 | tf_op jit(solution)/shard_map/slice | solution.py:47
  47.5 0.9 %convert_element_type.54 = f32[16,16,1,256]{3,0,2,1:T(8,128)S(1)} convert(bf16[16,16,1,256]{3,0,2,1:T(8,128)(2,1)} %collective-permute-done.1) | non-fusion elementwise | flops 65536 | bytes 393216 | tf_op jit(solution)/shard_map/convert_element_type | solution.py:41
  48.4 0.9 %convert_element_type.53 = f32[16,16,1,256]{3,0,2,1:T(8,128)S(1)} convert(bf16[16,16,1,256]{3,0,2,1:T(8,128)(2,1)} %collective-permute-done) | non-fusion elementwise | flops 65536 | bytes 393216 | tf_op jit(solution)/shard_map/convert_element_type | solution.py:40
  49.4 12.0 %fusion.3 = f32[16,16,16,256]{3,0,2,1:T(8,128)S(1)} fusion(f32[16,16,1,256]{3,0,2,1:T(8,128)S(1)} %convert_element_type.53, f32[16,16,15,256]{3,0,2,1:T(8,128)} %slice.182, f32[16,16,15,256]{3,0,2,1:T(8,128)} %slice.185, f32[16,16,1,256]{3,0,2,1:T(8,128)S(1)} %convert_element_type.54, f32[16,15,16,256]{3,0,2,1:T(8,128)} %fusion.9, ...), kind=kLoop, calls=%fused_computation.8 | loop fusion | flops 9437184 | bytes 29327360 | tf_op jit(solution)/shard_map/add | solution.py:53
  61.7 0.9 %broadcast_multiply_fusion = (f32[16,16,16,256]{3,0,2,1:T(8,128)S(1)}, f32[16,16,16,256]{3,0,2,1:T(8,128)S(1)}) fusion(f32[16,16,16,256]{3,0,2,1:T(8,128)S(1)} %get-tuple-element.54, f32[16,16,256]{2,1,0:T(8,128)S(1)} %copy-done.5, f32[16,16,256]{2,1,0:T(8,128)S(1)} %copy-done.4), kind=kLoop, calls=%fused_computation.18 | loop fusion | flops 2097152 | bytes 13107200 | tf_op jit(solution)/shard_map/mul | solution.py:37
  62.6 0.7 slice.248
  63.4 1.2 %slice.249 = bf16[16,16,1,256]{3,0,2,1:T(8,128)(2,1)} slice(f32[16,16,16,256]{3,0,2,1:T(8,128)S(1)} %get-tuple-element.32), slice={[0:16], [0:16], [0:1], [0:256]} | slice | bytes 262144 | tf_op jit(solution)/shard_map/slice | solution.py:38
  64.5 1.9 %collective-permute-start.2 = (bf16[16,16,1,256]{3,0,2,1:T(8,128)(2,1)}, bf16[16,16,1,256]{3,0,2,1:T(8,128)(2,1)}, u32[]{:S(2)}, u32[]{:S(2)}) collective-permute-start(bf16[16,16,1,256]{3,0,2,1:T(8,128)(2,1)} %slice.249), channel_id=1, source_target_pairs={{4,0},{8,4},{12,8},{16,12},{20,16},{24,20},{28,24},{0,28},{5,1},{9... | collective-permute-start | bytes 393224 | tf_op jit(solution)/shard_map/ppermute | solution.py:20
  66.6 1.8 %slice_multiply_fusion.1 = (f32[16,16,16,255]{3,0,2,1:T(8,128)S(1)}, f32[16,16,16,255]{3,0,2,1:T(8,128)S(1)}) fusion(f32[16,16,16,256]{3,0,2,1:T(8,128)S(1)} %get-tuple-element.54, f32[16,16,255]{2,1,0:T(8,128)S(1)} %copy-done.3, f32[16,16,255]{2,1,0:T(8,128)S(1)} %bitcast.52), kind=kLoop, calls=%fused_computation.1 | loop fusion | flops 2088960 | bytes 17233920 | tf_op jit(solution)/shard_map/mul | solution.py:26
  68.4 3.6 %fusion.8 = f32[16,15,16,256]{3,0,2,1:T(8,128)} fusion(f32[16,16,16,256]{3,0,2,1:T(8,128)S(1)} %get-tuple-element.54, f32[15,16,256]{2,1,0:T(8,128)} %slice_bitcast_fusion), kind=kLoop, calls=%fused_computation.15 | loop fusion | flops 1966080 | bytes 12042240 | tf_op jit(solution)/shard_map/mul | solution.py:47
  72.0 2.3 %slice.200 = f32[16,16,15,256]{3,0,2,1:T(8,128)} slice(f32[16,16,16,256]{3,0,2,1:T(8,128)S(1)} %copy-done.2), slice={[0:16], [0:16], [0:15], [0:256]} | slice | bytes 7864320 | tf_op jit(solution)/shard_map/slice | solution.py:41
  74.3 2.3 %slice.197 = f32[16,16,15,256]{3,0,2,1:T(8,128)} slice(f32[16,16,16,256]{3,0,2,1:T(8,128)S(1)} %get-tuple-element.32), slice={[0:16], [0:16], [1:16], [0:256]} | slice | bytes 7864320 | tf_op jit(solution)/shard_map/slice | solution.py:40
  76.7 0.9 %convert_element_type.58 = f32[16,16,1,256]{3,0,2,1:T(8,128)S(1)} convert(bf16[16,16,1,256]{3,0,2,1:T(8,128)(2,1)} %collective-permute-done.2) | non-fusion elementwise | flops 65536 | bytes 393216 | tf_op jit(solution)/shard_map/convert_element_type | solution.py:40
  77.6 0.9 %convert_element_type.59 = f32[16,16,1,256]{3,0,2,1:T(8,128)S(1)} convert(bf16[16,16,1,256]{3,0,2,1:T(8,128)(2,1)} %collective-permute-done.3) | non-fusion elementwise | flops 65536 | bytes 393216 | tf_op jit(solution)/shard_map/convert_element_type | solution.py:41
  78.5 8.9 %fusion.7 = f32[16,16,16,256]{3,0,2,1:T(8,128)S(1)} fusion(f32[16,16,1,256]{3,0,2,1:T(8,128)S(1)} %convert_element_type.58, f32[16,16,15,256]{3,0,2,1:T(8,128)} %slice.197, f32[16,16,15,256]{3,0,2,1:T(8,128)} %slice.200, f32[16,16,1,256]{3,0,2,1:T(8,128)S(1)} %convert_element_type.59, f32[16,15,16,256]{3,0,2,1:T(8,128)} %fusion.8, ...), kind=kLoop, calls=%fused_computation.13 | loop fusion | flops 9437184 | bytes 29327360 | tf_op jit(solution)/shard_map/add | solution.py:53
  87.5 4.4 %copy.22 = f32[16,16,16,256]{3,2,1,0:T(8,128)} copy(f32[16,16,16,256]{3,0,2,1:T(8,128)S(1)} %fusion.26) | data formatting | bytes 8388608 | tf_op jit(solution)/shard_map/scatter-add | solution.py:54
  (25 shorter events, 0.8 us)
Async XLA Ops:
  21.2 26.2 %collective-permute-start.1 = (bf16[16,16,1,256]{3,0,2,1:T(8,128)(2,1)}, bf16[16,16,1,256]{3,0,2,1:T(8,128)(2,1)}, u32[]{:S(2)}, u32[]{:S(2)}) collective-permute-start(bf16[16,16,1,256]{3,0,2,1:T(8,128)(2,1)} %slice.250), channel_id=1, source_target_pairs={{28,0},{0,4},{4,8},{8,12},{12,16},{16,20},{20,24},{24,28},{29,1},{... | collective-permute-start | bytes 393224 | tf_op jit(solution)/shard_map/ppermute | solution.py:20
  23.4 25.0 %collective-permute-start = (bf16[16,16,1,256]{3,0,2,1:T(8,128)(2,1)}, bf16[16,16,1,256]{3,0,2,1:T(8,128)(2,1)}, u32[]{:S(2)}, u32[]{:S(2)}) collective-permute-start(bf16[16,16,1,256]{3,0,2,1:T(8,128)(2,1)} %slice.251), channel_id=1, source_target_pairs={{4,0},{8,4},{12,8},{16,12},{20,16},{24,20},{28,24},{0,28},{5,1},{9... | collective-permute-start | bytes 393224 | tf_op jit(solution)/shard_map/ppermute | solution.py:20
  42.8 6.5 %copy-start = (f32[16,16,16,256]{3,2,1,0:T(8,128)S(1)}, f32[16,16,16,256]{3,2,1,0:T(8,128)}, u32[]{:S(2)}) copy-start(f32[16,16,16,256]{3,2,1,0:T(8,128)} %param.9) | copy-start | bytes 12582916
  49.3 12.0 %copy-start.6 = (bf16[64,16,256]{2,1,0:T(8,128)(2,1)S(1)}, bf16[64,16,256]{2,1,0:T(8,128)(2,1)}, u32[]{:S(2)}) copy-start(bf16[64,16,256]{2,1,0:T(8,128)(2,1)} %param.11) | copy-start | bytes 1572868
  49.4 12.0 %copy-start.7 = (s32[16]{0:T(128)S(1)}, s32[16]{0:T(128)}, u32[]{:S(2)}) copy-start(s32[16]{0:T(128)} %param.12) | copy-start | bytes 196
  49.4 12.3 %copy-start.4 = (f32[16,16,256]{2,1,0:T(8,128)S(1)}, f32[16,16,256]{2,1,0:T(8,128)}, u32[]{:S(2)}) copy-start(f32[16,16,256]{2,1,0:T(8,128)} %get-tuple-element.41) | copy-start | bytes 786436
  49.4 12.3 %copy-start.5 = (f32[16,16,256]{2,1,0:T(8,128)S(1)}, f32[16,16,256]{2,1,0:T(8,128)}, u32[]{:S(2)}) copy-start(f32[16,16,256]{2,1,0:T(8,128)} %get-tuple-element.44) | copy-start | bytes 786436
  61.7 4.9 %copy-start.3 = (f32[16,16,255]{2,1,0:T(8,128)S(1)}, f32[16,16,255]{2,1,0:T(8,128)}, u32[]{:S(2)}) copy-start(f32[16,16,255]{2,1,0:T(8,128)} %slice.202) | copy-start | bytes 783364
  62.6 3.9 %copy-start.1 = (f32[16,16,16,256]{3,0,2,1:T(8,128)}, f32[16,16,16,256]{3,0,2,1:T(8,128)S(1)}, u32[]{:S(2)}) copy-start(f32[16,16,16,256]{3,0,2,1:T(8,128)S(1)} %get-tuple-element.31) | copy-start | bytes 12582916
  64.5 12.1 %collective-permute-start.2 = (bf16[16,16,1,256]{3,0,2,1:T(8,128)(2,1)}, bf16[16,16,1,256]{3,0,2,1:T(8,128)(2,1)}, u32[]{:S(2)}, u32[]{:S(2)}) collective-permute-start(bf16[16,16,1,256]{3,0,2,1:T(8,128)(2,1)} %slice.249), channel_id=1, source_target_pairs={{4,0},{8,4},{12,8},{16,12},{20,16},{24,20},{28,24},{0,28},{5,1},{9... | collective-permute-start | bytes 393224 | tf_op jit(solution)/shard_map/ppermute | solution.py:20
  66.4 11.2 %collective-permute-start.3 = (bf16[16,16,1,256]{3,0,2,1:T(8,128)(2,1)}, bf16[16,16,1,256]{3,0,2,1:T(8,128)(2,1)}, u32[]{:S(2)}, u32[]{:S(2)}) collective-permute-start(bf16[16,16,1,256]{3,0,2,1:T(8,128)(2,1)} %slice.248), channel_id=1, source_target_pairs={{28,0},{0,4},{4,8},{8,12},{12,16},{16,20},{20,24},{24,28},{29,1},{... | collective-permute-start | bytes 393224 | tf_op jit(solution)/shard_map/ppermute | solution.py:20
  68.4 3.6 %copy-start.2 = (f32[16,16,16,256]{3,0,2,1:T(8,128)S(1)}, f32[16,16,16,256]{3,0,2,1:T(8,128)}, u32[]{:S(2)}) copy-start(f32[16,16,16,256]{3,0,2,1:T(8,128)} %copy-done.1) | copy-start | bytes 12582916
where the time goes:
time: 92.3 us; the launch traced here: 91.9 us
  other arithmetic  44.2 us (48%)
  local copies, waits for them, and re-layouts  22.7 us (25%)
  blocking collectives  14.2 us (15%)
  starting transfers between devices  6.75 us (7%)
  between operations  3.84 us (4%)
    add x2, other arithmetic, finish(): state = flat + vertical(lam, mixing)  20.8 us
    all_gather x2, blocking collectives, per_device(): metnow = lax.all_gather(locals_list[step], 'rcpt', axis=1, tiled=True)  14.2 us
    ppermute x4, starting transfers between devices, passed_along(): return lax.ppermute(block, axis, route)  6.75 us
    unnamed x1, other arithmetic  6.53 us
    mul x2, other arithmetic, vertical(): flux = coeff[:-1] * (lam[:, 1:] - lam[:, :-1])  6.15 us
    mul x2, other arithmetic, interior(): py = lam * jnp.maximum(cy, 0.0)  4.77 us
    slice x2, local copies, waits for them, and re-layouts, horizontal_shift(): east = jnp.concatenate([px[:, :, 1:], east_edge], axis=2)  4.69 us
    slice x2, local copies, waits for them, and re-layouts, horizontal_shift(): west = jnp.concatenate([west_edge, mx[:, :, :-1]], axis=2)  4.56 us
  transfers between devices with their start and end apart: 4, of which 0 were waited for; matrix products, arithmetic and copies ran while one was open for 29% of the time, Pallas kernels for 0%

commit v1 on v0

v1 whole, which is shorter than its diff:
```python
import functools

import jax
import jax.numpy as jnp
from jax import lax
from jax.experimental import pallas as pl
from jax.experimental.pallas import tpu as pltpu
from jax.sharding import PartitionSpec as P

STEPS = 2
F32 = jnp.float32
BF16 = jnp.bfloat16
MESH = pl.DeviceIdType.MESH


def mixing_of(m):
    return 0.02 + 0.25 * jnp.abs(m.astype(F32))


def shifted(x, by, axis):
    return pltpu.roll(x, (-by) % x.shape[axis], axis)


def latitude_coeffs(cy):
    lane = lax.broadcasted_iota(jnp.int32, cy.shape, 1)
    north = jnp.where(lane == cy.shape[1] - 1, 0.0, shifted(jnp.maximum(cy, 0.0), 1, 1))
    south = jnp.where(lane == 0, 0.0, shifted(-jnp.minimum(cy, 0.0), -1, 1))
    return north, south


def level_coeffs(met, k, levels):
    cx = met(0, k).astype(F32)
    cy = met(1, k).astype(F32)
    below = jnp.maximum(k - 1, 0)
    up = mixing_of(met(2, k)) * (k < levels - 1).astype(F32)
    down = mixing_of(met(2, below)) * (k > 0).astype(F32)
    row = lax.broadcasted_iota(jnp.int32, cx.shape, 0)
    east = jnp.where(row == cx.shape[0] - 1, 0.0, shifted(jnp.maximum(cx, 0.0), 1, 0))
    west = jnp.where(row == 0, 0.0, shifted(-jnp.minimum(cx, 0.0), -1, 0))
    north, south = latitude_coeffs(cy)
    centre = 1.0 - jnp.abs(cx) - jnp.abs(cy) - up - down
    return centre, up, down, east, west, north, south


def advance(lam, above, below, coeffs):
    centre, up, down, east, west, north, south = coeffs
    out = lam * centre + (above * up + below * down)
    out += shifted(lam, 1, 0) * east + shifted(lam, -1, 0) * west
    out += shifted(lam, 1, 1) * north + shifted(lam, -1, 1) * south
    return out


def first_step(
    tiles,
    ranks,
    hour_ref,
    ids_ref,
    lam_hbm,
    met_ref,
    forcing_ref,
    lam1_hbm,
    met1_ref,
    halo_ref,
    rows_ref,
    lam,
    lam1,
    met0,
    edges,
    lam_out,
    lam_in,
    cx_out,
    cx_in,
    flux_out,
    columns,
    lam_sem,
    out_sem,
    gsend,
    grecv,
    hsend,
    hrecv,
):
    tracers, levels, lons, _ = lam.shape
    share = levels // ranks
    tile, rank = lax.axis_index("tile"), lax.axis_index("rcpt")
    east, west = lax.rem(tile + 1, tiles), lax.rem(tile + tiles - 1, tiles)
    last = lons - 1

    load = pltpu.make_async_copy(lam_hbm, lam, lam_sem)
    load.start()

    bits = []
    b = ranks // 2
    while b:
        bits.append(b)
        b //= 2
    barrier = pltpu.get_barrier_semaphore()
    for other in (east, west):
        pl.semaphore_signal(barrier, inc=1, device_id=(other, rank), device_id_type=MESH)
    for b in bits:
        pl.semaphore_signal(barrier, inc=1, device_id=(tile, rank ^ b), device_id_type=MESH)

    mine = pl.ds(rank * share, share)
    met0[:, mine] = met_ref[hour_ref[0]]
    met1_ref[:, mine] = met_ref[hour_ref[1]]

    pl.semaphore_wait(barrier, 2 + len(bits))

    gathers = {}

    def send_block(step, offset, b):
        buf = (met0, met1_ref)[step]
        where = pl.ds((rank ^ offset) * share, share)
        copy = pltpu.make_async_remote_copy(
            src_ref=buf.at[:, where],
            dst_ref=buf.at[:, where],
            send_sem=gsend.at[step, offset ^ b],
            recv_sem=grecv.at[step, offset ^ b],
            device_id=(tile, rank ^ b),
            device_id_type=MESH,
        )
        copy.start()
        gathers[step, offset ^ b] = copy

    def arrived(step, offset):
        buf = (met0, met1_ref)[step]
        where = pl.ds((rank ^ offset) * share, share)
        pltpu.make_async_remote_copy(
            src_ref=buf.at[:, where],
            dst_ref=buf.at[:, where],
            send_sem=gsend.at[step, offset],
            recv_sem=grecv.at[step, offset],
            device_id=(tile, rank ^ offset),
            device_id_type=MESH,
        ).wait_recv()

    def spread(step, offset, after):
        for i in range(after, len(bits)):
            send_block(step, offset, bits[i])

    def forward(step):
        for offset in order:
            arrived(step, offset)
            low = offset & -offset
            spread(step, offset, bits.index(low) + 1)

    order = sorted(range(1, ranks), key=lambda o: (bin(o).count("1"), -o))

    spread(0, 0, 0)

    load.wait()

    def pick(t, _):
        for n, c in enumerate((0, 1, last - 1, last)):
            edges[n, t] = lam[t, :, c, :]
        lam_out[0, t] = edges[0, t].astype(BF16)
        lam_out[1, t] = edges[3, t].astype(BF16)
        return 0

    lax.fori_loop(0, tracers, pick, 0)

    def halo_copy(n, src, dst, side):
        return pltpu.make_async_remote_copy(
            src_ref=src.at[side],
            dst_ref=dst.at[side],
            send_sem=hsend.at[n, side],
            recv_sem=hrecv.at[n, side],
            device_id=((west, east)[side], rank),
            device_id_type=MESH,
        )

    lam_copies = [halo_copy(0, lam_out, lam_in, side) for side in (0, 1)]
    for c in lam_copies:
        c.start()

    def source(t, _):
        rows_ref[t] = forcing_ref[ids_ref[t]]
        return 0

    lax.fori_loop(0, tracers, source, 0)

    forward(0)
    spread(1, 0, 0)

    def pick_met(k, _):
        cx = met0[0, k].astype(F32)
        cy = met0[1, k].astype(F32)
        kz = met0[2, k].astype(F32)
        rows = [cx[0:1], cx[1:2], cx[last - 1 : last], cx[last : last + 1]]
        rows += [cy[0:1], cy[last : last + 1], kz[0:1], kz[last : last + 1]]
        for n, r in enumerate(rows):
            columns[n, pl.ds(k, 1), :] = r
        return 0

    lax.fori_loop(0, levels, pick_met, 0)
    cx_out[0] = columns[0].astype(BF16)
    cx_out[1] = columns[3].astype(BF16)
    cx_copies = [halo_copy(1, cx_out, cx_in, side) for side in (0, 1)]
    for c in cx_copies:
        c.start()

    group = 4 if tracers % 4 == 0 else 1

    def level(k, _):
        coeffs = level_coeffs(lambda f, n: met0[f, n], k, levels)
        above = jnp.minimum(k + 1, levels - 1)
        below = jnp.maximum(k - 1, 0)

        def some(g, _):
            for u in range(group):
                t = g * group + u
                lam1[t, k] = advance(lam[t, k], lam[t, above], lam[t, below], coeffs)
            return 0

        lax.fori_loop(0, tracers // group, some, 0)
        return 0

    lax.fori_loop(0, levels, level, 0)

    def add_rows(t, _):
        lam1[t, levels - 1] += rows_ref[t].astype(F32)
        return 0

    lax.fori_loop(0, tracers, add_rows, 0)

    forward(1)

    def pick_next(k, _):
        cx = met1_ref[0, k].astype(F32)
        columns[8, pl.ds(k, 1), :] = cx[0:1]
        columns[9, pl.ds(k, 1), :] = cx[last : last + 1]
        return 0

    lax.fori_loop(0, levels, pick_next, 0)

    for c in cx_copies + lam_copies:
        c.wait()

    def edge_coeffs(side):
        cx = columns[(0, 3)[side]]
        cy = columns[4 + side]
        kz = mixing_of(columns[6 + side])
        row = lax.broadcasted_iota(jnp.int32, kz.shape, 0)
        up = jnp.where(row == levels - 1, 0.0, kz)
        down = shifted(up, -1, 0)
        north, south = latitude_coeffs(cy)
        if side == 0:
            from_east = jnp.maximum(columns[1], 0.0)
            from_west = -jnp.minimum(cx_in[1].astype(F32), 0.0)
            leaves = jnp.maximum(columns[8], 0.0)
        else:
            from_east = jnp.maximum(cx_in[0].astype(F32), 0.0)
            from_west = -jnp.minimum(columns[2], 0.0)
            leaves = -jnp.minimum(columns[9], 0.0)
        centre = 1.0 - jnp.abs(cx) - jnp.abs(cy) - up - down
        return centre, up, down, from_east, from_west, north, south, leaves

    flux_copies = []
    for side in (0, 1):
        centre, up, down, from_east, from_west, north, south, leaves = edge_coeffs(side)
        top = lax.broadcasted_iota(jnp.int32, centre.shape, 0) == levels - 1
        c = (0, last)[side]

        def edge(t, _):
            x = edges[(0, 3)[side], t]
            if side == 0:
                e, w = edges[1, t], lam_in[1, t].astype(F32)
            else:
                e, w = lam_in[0, t].astype(F32), edges[2, t]
            out = x * centre + shifted(x, 1, 0) * up + shifted(x, -1, 0) * down
            out += e * from_east + w * from_west
            out += shifted(x, 1, 1) * north + shifted(x, -1, 1) * south
            out += jnp.where(top, rows_ref[t].astype(F32)[c : c + 1], 0.0)
            flux_out[side, t] = (out * leaves).astype(BF16)
            lam1[t, :, c, :] = out
            return 0

        lax.fori_loop(0, tracers, edge, 0)
        copy = halo_copy(2, flux_out, halo_ref, side)
        copy.start()
        flux_copies.append(copy)

    store = pltpu.make_async_copy(lam1, lam1_hbm, out_sem)
    store.start()
    for copy in gathers.values():
        copy.wait_send()
    for copy in flux_copies:
        copy.wait()
    store.wait()


def second_step(lam_ref, met_ref, halo_ref, rows_ref, out_ref, halo):
    tracers, levels, lons, _ = lam_ref.shape
    halo[...] = halo_ref[...].astype(F32)
    row = lax.broadcasted_iota(jnp.int32, lam_ref.shape[2:], 0)

    def level(k, _):
        coeffs = level_coeffs(lambda f, n: met_ref[f, n], k, levels)
        above = jnp.minimum(k + 1, levels - 1)
        below = jnp.maximum(k - 1, 0)
        for t in range(tracers):
            out = advance(lam_ref[t, k], lam_ref[t, above], lam_ref[t, below], coeffs)
            out += jnp.where(row == lons - 1, halo[0, t, pl.ds(k, 1), :], 0.0)
            out += jnp.where(row == 0, halo[1, t, pl.ds(k, 1), :], 0.0)
            out_ref[t, k] = out
        return 0

    lax.fori_loop(0, levels, level, 0)
    for t in range(tracers):
        out_ref[t, levels - 1] += rows_ref[t].astype(F32)


def per_device(tiles, ranks, adjoint_state, met_fields, forcing, cluster_ids, hour_index):
    tracers, levels, lons, lats = adjoint_state.shape
    fields = met_fields.shape[1]
    vmem = pl.BlockSpec(memory_space=pltpu.VMEM)
    smem = pl.BlockSpec(memory_space=pltpu.SMEM)
    hbm = pl.BlockSpec(memory_space=pl.ANY)
    both = (2, tracers, levels, lats)
    lam1, met1, halo, rows = pl.pallas_call(
        functools.partial(first_step, tiles, ranks),
        out_shape=(
            jax.ShapeDtypeStruct(adjoint_state.shape, F32),
            jax.ShapeDtypeStruct((fields, levels, lons, lats), BF16),
            jax.ShapeDtypeStruct(both, BF16),
            jax.ShapeDtypeStruct((tracers, lons, lats), BF16),
        ),
        in_specs=[smem, smem, hbm, vmem, vmem],
        out_specs=(hbm, vmem, vmem, vmem),
        scratch_shapes=[
            pltpu.VMEM(adjoint_state.shape, F32),
            pltpu.VMEM(adjoint_state.shape, F32),
            pltpu.VMEM((fields, levels, lons, lats), BF16),
            pltpu.VMEM((4, tracers, levels, lats), F32),
            pltpu.VMEM(both, BF16),
            pltpu.VMEM(both, BF16),
            pltpu.VMEM((2, levels, lats), BF16),
            pltpu.VMEM((2, levels, lats), BF16),
            pltpu.VMEM(both, BF16),
            pltpu.VMEM((10, levels, lats), F32),
            pltpu.SemaphoreType.DMA,
            pltpu.SemaphoreType.DMA,
            pltpu.SemaphoreType.DMA((STEPS, ranks)),
            pltpu.SemaphoreType.DMA((STEPS, ranks)),
            pltpu.SemaphoreType.DMA((3, 2)),
            pltpu.SemaphoreType.DMA((3, 2)),
        ],
        compiler_params=pltpu.CompilerParams(
            collective_id=0, has_side_effects=True, vmem_limit_bytes=40 << 20
        ),
        name="first_step",
    )(hour_index, cluster_ids, adjoint_state, met_fields, forcing)

    block = 4 if tracers % 4 == 0 else 1
    state = pl.BlockSpec((block, levels, lons, lats), lambda t: (t, 0, 0, 0))
    return pl.pallas_call(
        second_step,
        grid=(tracers // block,),
        out_shape=jax.ShapeDtypeStruct(adjoint_state.shape, F32),
        in_specs=[
            state,
            pl.BlockSpec(met1.shape, lambda t: (0, 0, 0, 0)),
            pl.BlockSpec((2, block, levels, lats), lambda t: (0, t, 0, 0)),
            pl.BlockSpec((block, lons, lats), lambda t: (t, 0, 0)),
        ],
        out_specs=state,
        scratch_shapes=[pltpu.VMEM((2, block, levels, lats), F32)],
        compiler_params=pltpu.CompilerParams(vmem_limit_bytes=40 << 20),
        name="second_step",
    )(lam1, met1, halo, rows)


def solution(mesh):
    placed = (
        P("rcpt", None, "tile", None),
        P(None, None, "rcpt", "tile", None),
        P(None, "tile", None),
        P("rcpt"),
        P(),
    )
    return jax.shard_map(
        functools.partial(per_device, mesh.shape["tile"], mesh.shape["rcpt"]),
        mesh=mesh,
        in_specs=placed,
        out_specs=P("rcpt", None, "tile", None),
        check_vma=False,
    )
```

time: 92.3 us -> 43.8 us (0.47)
  other arithmetic: 44.2 us -> 0 us
  Pallas kernels: 0 us -> 37.7 us
  local copies, waits for them, and re-layouts: 22.7 us -> 5.81 us
  blocking collectives: 14.2 us -> 0 us
  starting transfers between devices: 6.75 us -> 0 us
  between operations: 3.84 us -> 0.01 us
    pallas_call x0 -> x2, Pallas kernels: none -> 37.7 us  [the longest x1 28.8 us: per_device(): pl.pallas_call(functools.partial(first_step, tiles, ranks), out_shape=(ja...]
    add x2 -> x0, other arithmetic: 20.8 us -> none  [finish(): state = flat + vertical(lam, mixing)]
    slice x13 -> x0, local copies, waits for them, and re-layouts: 17.2 us -> none  [the longest x2 4.69 us: horizontal_shift(): east = jnp.concatenate([px[:, :, 1:], east_edge], axis=2)]
    all_gather x2 -> x0, blocking collectives: 14.2 us -> none  [per_device(): metnow = lax.all_gather(locals_list[step], 'rcpt', axis=1, tiled=True)]
    mul x7 -> x0, other arithmetic: 13 us -> none  [the longest x2 6.15 us: vertical(): flux = coeff[:-1] * (lam[:, 1:] - lam[:, :-1])]
    ppermute x4 -> x0, starting transfers between devices: 6.75 us -> none  [passed_along(): return lax.ppermute(block, axis, route)]
    unnamed x1 -> x0, other arithmetic: 6.53 us -> none
    unnamed x16 -> x10, local copies, waits for them, and re-layouts: 0.04 us -> 5.81 us
  transfers between devices with their start and end apart: 4 -> 0, of which waited for: 0 -> 0; matrix products, arithmetic and copies ran while one was open for 29% -> 0% of each run, Pallas kernels for 0% -> 0%
where the time goes in v1:
time: 43.8 us; the launch traced here: 43.5 us
  Pallas kernels  37.7 us (86%)
  local copies, waits for them, and re-layouts  5.81 us (13%)
    pallas_call x1, Pallas kernels, per_device(): pl.pallas_call(functools.partial(first_step, tiles, ranks), out_shape=(ja...  28.8 us
    pallas_call x1, Pallas kernels, per_device(): pl.pallas_call(second_step, grid=(tracers // block,), out_shape=jax.Shape...  8.92 us
    unnamed x10, local copies, waits for them, and re-layouts  5.81 us

profile of v1, /device:TPU:0, one launch (start us, length us, event | category | flops | bytes accessed | tf_op | source)
XLA Modules:
  0.0 43.5 jit_solution(558683663938035145)
XLA Ops:
  0.0 0.0 copy-start
  0.0 2.2 %copy-done = f32[16,16,16,256]{3,2,1,0:T(8,128)S(1)} copy-done((f32[16,16,16,256]{3,2,1,0:T(8,128)S(1)}, f32[16,16,16,256]{3,2,1,0:T(8,128)}, u32[]{:S(2)}) %copy-start) | copy-done | bytes 4194328
  2.2 0.0 copy-start.1
  2.2 1.3 %copy-done.1 = bf16[12,3,4,16,256]{4,3,2,1,0:T(8,128)(2,1)S(1)} copy-done((bf16[12,3,4,16,256]{4,3,2,1,0:T(8,128)(2,1)S(1)}, bf16[12,3,4,16,256]{4,3,2,1,0:T(8,128)(2,1)}, u32[]{:S(2)}) %copy-start.1) | copy-done | bytes 1179672
  3.5 0.0 copy-start.2
  3.5 1.0 %copy-done.2 = bf16[64,16,256]{2,1,0:T(8,128)(2,1)S(1)} copy-done((bf16[64,16,256]{2,1,0:T(8,128)(2,1)S(1)}, bf16[64,16,256]{2,1,0:T(8,128)(2,1)}, u32[]{:S(2)}) %copy-start.2) | copy-done | bytes 524312
  4.5 0.0 copy-start.3
  4.5 0.7 %copy-done.3 = s32[2]{0:T(128)S(1)} copy-done((s32[2]{0:T(128)S(1)}, s32[2]{0:T(128)}, u32[]{:S(2)}) %copy-start.3) | copy-done | bytes 32
  5.2 0.0 copy-start.4
  5.2 0.7 %copy-done.4 = s32[16]{0:T(128)S(1)} copy-done((s32[16]{0:T(128)S(1)}, s32[16]{0:T(128)}, u32[]{:S(2)}) %copy-start.4) | copy-done | bytes 88
  5.8 28.8 %first_step.1 = (f32[16,16,16,256]{3,2,1,0:T(8,128)S(1)}, bf16[3,16,16,256]{3,2,1,0:T(8,128)(2,1)S(1)}, bf16[2,16,16,256]{3,2,1,0:T(8,128)(2,1)S(1)}, bf16[16,16,256]{2,1,0:T(8,128)(2,1)S(1)}) custom-call(s32[2]{0:T(128)S(1)} %copy-done.3, s32[16]{0:T(128)S(1)} %copy-done.4, f32[16,16,16,256]{3,2,1,0:T(8,128)S(1)} %copy-done, ...), custom_call_target="tpu_custom_call" | custom-call | tf_op jit(solution)/shard_map/first_step/pallas_call | solution.py:319
  34.6 8.9 %second_step.1 = f32[16,16,16,256]{3,2,1,0:T(8,128)} custom-call(f32[16,16,16,256]{3,2,1,0:T(8,128)S(1)} %get-tuple-element.9.lam_ref, bf16[3,16,16,256]{3,2,1,0:T(8,128)(2,1)S(1)} %get-tuple-element.10.met_ref, bf16[2,16,16,256]{3,2,1,0:T(8,128)(2,1)S(1)} %get-tuple-element.11.halo_ref, bf16[16,16,256]{2,1,0:T(8,128)(2,1)S(1)} %get-tuple-element.12.rows_ref), custom_call_target="tpu_custom_call" | custom-call | tf_op jit(solution)/shard_map/second_step/pallas_call | solution.py:355
Async XLA Ops:
  0.0 2.2 %copy-start = (f32[16,16,16,256]{3,2,1,0:T(8,128)S(1)}, f32[16,16,16,256]{3,2,1,0:T(8,128)}, u32[]{:S(2)}) copy-start(f32[16,16,16,256]{3,2,1,0:T(8,128)} %lam_hbm.1) | copy-start | bytes 12582916
  2.2 1.3 %copy-start.1 = (bf16[12,3,4,16,256]{4,3,2,1,0:T(8,128)(2,1)S(1)}, bf16[12,3,4,16,256]{4,3,2,1,0:T(8,128)(2,1)}, u32[]{:S(2)}) copy-start(bf16[12,3,4,16,256]{4,3,2,1,0:T(8,128)(2,1)} %met_ref.1) | copy-start | bytes 3538948
  3.5 1.0 %copy-start.2 = (bf16[64,16,256]{2,1,0:T(8,128)(2,1)S(1)}, bf16[64,16,256]{2,1,0:T(8,128)(2,1)}, u32[]{:S(2)}) copy-start(bf16[64,16,256]{2,1,0:T(8,128)(2,1)} %forcing_ref.1) | copy-start | bytes 1572868
  4.5 0.7 %copy-start.3 = (s32[2]{0:T(128)S(1)}, s32[2]{0:T(128)}, u32[]{:S(2)}) copy-start(s32[2]{0:T(128)} %hour_ref.1) | copy-start | bytes 28
  5.2 0.7 %copy-start.4 = (s32[16]{0:T(128)S(1)}, s32[16]{0:T(128)}, u32[]{:S(2)}) copy-start(s32[16]{0:T(128)} %ids_ref.1) | copy-start | bytes 196

commit v2 on v1

--- a/solution.py
+++ b/solution.py
@@ -53,17 +53,20 @@
 def first_step(
     tiles,
     ranks,
-    hour_ref,
-    ids_ref,
+    hour_hbm,
+    ids_hbm,
     lam_hbm,
-    met_ref,
-    forcing_ref,
-    lam1_hbm,
+    met_hbm,
+    forcing_hbm,
+    lam1,
     met1_ref,
     halo_ref,
     rows_ref,
+    hour_ref,
+    ids_ref,
     lam,
-    lam1,
+    met_ref,
+    forcing_ref,
     met0,
     edges,
     lam_out,
@@ -72,8 +75,7 @@
     cx_in,
     flux_out,
     columns,
-    lam_sem,
-    out_sem,
+    load_sem,
     gsend,
     grecv,
     hsend,
@@ -85,8 +87,11 @@
     east, west = lax.rem(tile + 1, tiles), lax.rem(tile + tiles - 1, tiles)
     last = lons - 1
 
-    load = pltpu.make_async_copy(lam_hbm, lam, lam_sem)
-    load.start()
+    pairs = ((hour_hbm, hour_ref), (met_hbm, met_ref), (lam_hbm, lam))
+    pairs += ((ids_hbm, ids_ref), (forcing_hbm, forcing_ref))
+    loads = [pltpu.make_async_copy(*pair, load_sem.at[n]) for n, pair in enumerate(pairs)]
+    for load in loads:
+        load.start()
 
     bits = []
     b = ranks // 2
@@ -99,6 +104,8 @@
     for b in bits:
         pl.semaphore_signal(barrier, inc=1, device_id=(tile, rank ^ b), device_id_type=MESH)
 
+    loads[0].wait()
+    loads[1].wait()
     mine = pl.ds(rank * share, share)
     met0[:, mine] = met_ref[hour_ref[0]]
     met1_ref[:, mine] = met_ref[hour_ref[1]]
@@ -137,17 +144,19 @@
         for i in range(after, len(bits)):
             send_block(step, offset, bits[i])
 
-    def forward(step):
-        for offset in order:
+    def forward(step, which):
+        for offset in which:
             arrived(step, offset)
             low = offset & -offset
             spread(step, offset, bits.index(low) + 1)
 
     order = sorted(range(1, ranks), key=lambda o: (bin(o).count("1"), -o))
+    passed_on = [o for o in order if o % 2 == 0]
+    kept = [o for o in order if o % 2]
 
     spread(0, 0, 0)
 
-    load.wait()
+    loads[2].wait()
 
     def pick(t, _):
         for n, c in enumerate((0, 1, last - 1, last)):
@@ -172,13 +181,16 @@
     for c in lam_copies:
         c.start()
 
+    loads[3].wait()
+    loads[4].wait()
+
     def source(t, _):
         rows_ref[t] = forcing_ref[ids_ref[t]]
         return 0
 
     lax.fori_loop(0, tracers, source, 0)
 
-    forward(0)
+    forward(0, order)
     spread(1, 0, 0)
 
     def pick_met(k, _):
@@ -214,7 +226,9 @@
         lax.fori_loop(0, tracers // group, some, 0)
         return 0
 
-    lax.fori_loop(0, levels, level, 0)
+    lax.fori_loop(0, levels // 2, level, 0)
+    forward(1, passed_on)
+    lax.fori_loop(levels // 2, levels, level, 0)
 
     def add_rows(t, _):
         lam1[t, levels - 1] += rows_ref[t].astype(F32)
@@ -222,7 +236,7 @@
 
     lax.fori_loop(0, tracers, add_rows, 0)
 
-    forward(1)
+    forward(1, kept)
 
     def pick_next(k, _):
         cx = met1_ref[0, k].astype(F32)
@@ -279,18 +293,17 @@
         copy.start()
         flux_copies.append(copy)
 
-    store = pltpu.make_async_copy(lam1, lam1_hbm, out_sem)
-    store.start()
     for copy in gathers.values():
         copy.wait_send()
     for copy in flux_copies:
         copy.wait()
-    store.wait()
 
 
 def second_step(lam_ref, met_ref, halo_ref, rows_ref, out_ref, halo):
-    tracers, levels, lons, _ = lam_ref.shape
-    halo[...] = halo_ref[...].astype(F32)
+    _, levels, lons, _ = lam_ref.shape
+    tracers = out_ref.shape[0]
+    first = pl.program_id(0) * tracers
+    halo[...] = halo_ref[:, pl.ds(first, tracers)].astype(F32)
     row = lax.broadcasted_iota(jnp.int32, lam_ref.shape[2:], 0)
 
     def level(k, _):
@@ -298,7 +311,8 @@
         above = jnp.minimum(k + 1, levels - 1)
         below = jnp.maximum(k - 1, 0)
         for t in range(tracers):
-            out = advance(lam_ref[t, k], lam_ref[t, above], lam_ref[t, below], coeffs)
+            x = lam_ref[first + t, k]
+            out = advance(x, lam_ref[first + t, above], lam_ref[first + t, below], coeffs)
             out += jnp.where(row == lons - 1, halo[0, t, pl.ds(k, 1), :], 0.0)
             out += jnp.where(row == 0, halo[1, t, pl.ds(k, 1), :], 0.0)
             out_ref[t, k] = out
@@ -306,16 +320,17 @@
 
     lax.fori_loop(0, levels, level, 0)
     for t in range(tracers):
-        out_ref[t, levels - 1] += rows_ref[t].astype(F32)
+        out_ref[t, levels - 1] += rows_ref[first + t].astype(F32)
 
 
 def per_device(tiles, ranks, adjoint_state, met_fields, forcing, cluster_ids, hour_index):
     tracers, levels, lons, lats = adjoint_state.shape
     fields = met_fields.shape[1]
     vmem = pl.BlockSpec(memory_space=pltpu.VMEM)
-    smem = pl.BlockSpec(memory_space=pltpu.SMEM)
-    hbm = pl.BlockSpec(memory_space=pl.ANY)
+    hbm = pl.BlockSpec(memory_space=pltpu.HBM)
     both = (2, tracers, levels, lats)
+    arrays = (hour_index, cluster_ids, adjoint_state, met_fields, forcing)
+    arrays = [pltpu.with_memory_space_constraint(x, pltpu.HBM) for x in arrays]
     lam1, met1, halo, rows = pl.pallas_call(
         functools.partial(first_step, tiles, ranks),
         out_shape=(
@@ -324,11 +339,14 @@
             jax.ShapeDtypeStruct(both, BF16),
             jax.ShapeDtypeStruct((tracers, lons, lats), BF16),
         ),
-        in_specs=[smem, smem, hbm, vmem, vmem],
-        out_specs=(hbm, vmem, vmem, vmem),
+        in_specs=[hbm] * 5,
+        out_specs=(vmem,) * 4,
         scratch_shapes=[
+            pltpu.SMEM(hour_index.shape, jnp.int32),
+            pltpu.SMEM(cluster_ids.shape, jnp.int32),
             pltpu.VMEM(adjoint_state.shape, F32),
-            pltpu.VMEM(adjoint_state.shape, F32),
+            pltpu.VMEM(met_fields.shape, BF16),
+            pltpu.VMEM(forcing.shape, BF16),
             pltpu.VMEM((fields, levels, lons, lats), BF16),
             pltpu.VMEM((4, tracers, levels, lats), F32),
             pltpu.VMEM(both, BF16),
@@ -337,8 +355,7 @@
             pltpu.VMEM((2, levels, lats), BF16),
             pltpu.VMEM(both, BF16),
             pltpu.VMEM((10, levels, lats), F32),
-            pltpu.SemaphoreType.DMA,
-            pltpu.SemaphoreType.DMA,
+            pltpu.SemaphoreType.DMA((5,)),
             pltpu.SemaphoreType.DMA((STEPS, ranks)),
             pltpu.SemaphoreType.DMA((STEPS, ranks)),
             pltpu.SemaphoreType.DMA((3, 2)),
@@ -348,7 +365,7 @@
             collective_id=0, has_side_effects=True, vmem_limit_bytes=40 << 20
         ),
         name="first_step",
-    )(hour_index, cluster_ids, adjoint_state, met_fields, forcing)
+    )(*arrays)
 
     block = 4 if tracers % 4 == 0 else 1
     state = pl.BlockSpec((block, levels, lons, lats), lambda t: (t, 0, 0, 0))
@@ -356,12 +373,7 @@
         second_step,
         grid=(tracers // block,),
         out_shape=jax.ShapeDtypeStruct(adjoint_state.shape, F32),
-        in_specs=[
-            state,
-            pl.BlockSpec(met1.shape, lambda t: (0, 0, 0, 0)),
-            pl.BlockSpec((2, block, levels, lats), lambda t: (0, t, 0, 0)),
-            pl.BlockSpec((block, lons, lats), lambda t: (t, 0, 0)),
-        ],
+        in_specs=[vmem] * 4,
         out_specs=state,
         scratch_shapes=[pltpu.VMEM((2, block, levels, lats), F32)],
         compiler_params=pltpu.CompilerParams(vmem_limit_bytes=40 << 20),

time: 43.8 us -> 36.4 us (0.83)
  local copies, waits for them, and re-layouts: 5.81 us -> 0 us
  Pallas kernels: 37.7 us -> 36.2 us
    unnamed x10 -> x0, local copies, waits for them, and re-layouts: 5.81 us -> none
    pallas_call x1, Pallas kernels: 28.8 us -> 27.3 us  [per_device(): pl.pallas_call(functools.partial(first_step, tiles, ranks), out_shape=(ja...]
where the time goes in v2:
time: 36.4 us; the launch traced here: 36.2 us
  Pallas kernels  36.2 us (99%)
    pallas_call x1, Pallas kernels, per_device(): pl.pallas_call(functools.partial(first_step, tiles, ranks), out_shape=(ja...  27.3 us
    pallas_call x1, Pallas kernels, per_device(): pl.pallas_call(second_step, grid=(tracers // block,), out_shape=jax.Shape...  8.88 us

profile of v2, /device:TPU:0, one launch (start us, length us, event | category | flops | bytes accessed | tf_op | source)
XLA Modules:
  0.0 36.2 jit_solution(4968864195318503513)
XLA Ops:
  0.0 27.3 %first_step.1 = (f32[16,16,16,256]{3,2,1,0:T(8,128)S(1)}, bf16[3,16,16,256]{3,2,1,0:T(8,128)(2,1)S(1)}, bf16[2,16,16,256]{3,2,1,0:T(8,128)(2,1)S(1)}, bf16[16,16,256]{2,1,0:T(8,128)(2,1)S(1)}) custom-call(s32[2]{0:T(128)} %hour_hbm.1, s32[16]{0:T(128)} %ids_hbm.1, f32[16,16,16,256]{3,2,1,0:T(8,128)} %lam_hbm.1, bf16[12,3,4,16,256]{4,3,2,1,0:T(8,128)(2,1)} %met_hbm.1, ...), custom_call_target="tpu_custom_call" | custom-call | tf_op jit(solution)/shard_map/first_step/pallas_call | solution.py:334
  27.3 8.9 %second_step.1 = f32[16,16,16,256]{3,2,1,0:T(8,128)} custom-call(f32[16,16,16,256]{3,2,1,0:T(8,128)S(1)} %get-tuple-element.9.lam_ref, bf16[3,16,16,256]{3,2,1,0:T(8,128)(2,1)S(1)} %get-tuple-element.10.met_ref, bf16[2,16,16,256]{3,2,1,0:T(8,128)(2,1)S(1)} %get-tuple-element.11.halo_ref, bf16[16,16,256]{2,1,0:T(8,128)(2,1)S(1)} %get-tuple-element.12.rows_ref), custom_call_target="tpu_custom_call" | custom-call | tf_op jit(solution)/shard_map/second_step/pallas_call | solution.py:372

commit v3 on v2

--- a/solution.py
+++ b/solution.py
@@ -87,8 +87,12 @@
     east, west = lax.rem(tile + 1, tiles), lax.rem(tile + tiles - 1, tiles)
     last = lons - 1
 
-    pairs = ((hour_hbm, hour_ref), (met_hbm, met_ref), (lam_hbm, lam))
-    pairs += ((ids_hbm, ids_ref), (forcing_hbm, forcing_ref))
+    parts = 4 if tracers % 4 == 0 else 1
+    some = tracers // parts
+    cuts = [pl.ds(n * some, some) for n in range(parts)]
+    pairs = [(hour_hbm, hour_ref), (met_hbm, met_ref), (ids_hbm, ids_ref)]
+    pairs += [(lam_hbm.at[cut], lam.at[cut]) for cut in cuts]
+    pairs += [(forcing_hbm, forcing_ref)]
     loads = [pltpu.make_async_copy(*pair, load_sem.at[n]) for n, pair in enumerate(pairs)]
     for load in loads:
         load.start()
@@ -156,8 +160,6 @@
 
     spread(0, 0, 0)
 
-    loads[2].wait()
-
     def pick(t, _):
         for n, c in enumerate((0, 1, last - 1, last)):
             edges[n, t] = lam[t, :, c, :]
@@ -165,7 +167,9 @@
         lam_out[1, t] = edges[3, t].astype(BF16)
         return 0
 
-    lax.fori_loop(0, tracers, pick, 0)
+    for n in range(parts):
+        loads[3 + n].wait()
+        lax.fori_loop(n * some, (n + 1) * some, pick, 0, unroll=True)
 
     def halo_copy(n, src, dst, side):
         return pltpu.make_async_remote_copy(
@@ -181,14 +185,14 @@
     for c in lam_copies:
         c.start()
 
-    loads[3].wait()
-    loads[4].wait()
+    loads[2].wait()
+    loads[-1].wait()
 
     def source(t, _):
         rows_ref[t] = forcing_ref[ids_ref[t]]
         return 0
 
-    lax.fori_loop(0, tracers, source, 0)
+    lax.fori_loop(0, tracers, source, 0, unroll=True)
 
     forward(0, order)
     spread(1, 0, 0)
@@ -203,27 +207,23 @@
             columns[n, pl.ds(k, 1), :] = r
         return 0
 
-    lax.fori_loop(0, levels, pick_met, 0)
+    lax.fori_loop(0, levels, pick_met, 0, unroll=True)
     cx_out[0] = columns[0].astype(BF16)
     cx_out[1] = columns[3].astype(BF16)
     cx_copies = [halo_copy(1, cx_out, cx_in, side) for side in (0, 1)]
     for c in cx_copies:
         c.start()
 
-    group = 4 if tracers % 4 == 0 else 1
-
     def level(k, _):
         coeffs = level_coeffs(lambda f, n: met0[f, n], k, levels)
         above = jnp.minimum(k + 1, levels - 1)
         below = jnp.maximum(k - 1, 0)
 
-        def some(g, _):
-            for u in range(group):
-                t = g * group + u
-                lam1[t, k] = advance(lam[t, k], lam[t, above], lam[t, below], coeffs)
+        def one(t, _):
+            lam1[t, k] = advance(lam[t, k], lam[t, above], lam[t, below], coeffs)
             return 0
 
-        lax.fori_loop(0, tracers // group, some, 0)
+        lax.fori_loop(0, tracers, one, 0, unroll=True)
         return 0
 
     lax.fori_loop(0, levels // 2, level, 0)
@@ -234,7 +234,7 @@
         lam1[t, levels - 1] += rows_ref[t].astype(F32)
         return 0
 
-    lax.fori_loop(0, tracers, add_rows, 0)
+    lax.fori_loop(0, tracers, add_rows, 0, unroll=True)
 
     forward(1, kept)
 
@@ -244,7 +244,7 @@
         columns[9, pl.ds(k, 1), :] = cx[last : last + 1]
         return 0
 
-    lax.fori_loop(0, levels, pick_next, 0)
+    lax.fori_loop(0, levels, pick_next, 0, unroll=True)
 
     for c in cx_copies + lam_copies:
         c.wait()
@@ -288,7 +288,7 @@
             lam1[t, :, c, :] = out
             return 0
 
-        lax.fori_loop(0, tracers, edge, 0)
+        lax.fori_loop(0, tracers, edge, 0, unroll=True)
         copy = halo_copy(2, flux_out, halo_ref, side)
         copy.start()
         flux_copies.append(copy)
@@ -300,27 +300,34 @@
 
 
 def second_step(lam_ref, met_ref, halo_ref, rows_ref, out_ref, halo):
-    _, levels, lons, _ = lam_ref.shape
-    tracers = out_ref.shape[0]
-    first = pl.program_id(0) * tracers
-    halo[...] = halo_ref[:, pl.ds(first, tracers)].astype(F32)
+    tracers, levels, lons, _ = lam_ref.shape
+    held = out_ref.shape[1]
+    step = pl.program_id(0)
+
+    @pl.when(step == 0)
+    def _():
+        halo[...] = halo_ref[...].astype(F32)
+
     row = lax.broadcasted_iota(jnp.int32, lam_ref.shape[2:], 0)
 
-    def level(k, _):
-        coeffs = level_coeffs(lambda f, n: met_ref[f, n], k, levels)
+    def level(n, _):
+        k = step * held + n
+        coeffs = level_coeffs(lambda f, m: met_ref[f, m], k, levels)
         above = jnp.minimum(k + 1, levels - 1)
         below = jnp.maximum(k - 1, 0)
         for t in range(tracers):
-            x = lam_ref[first + t, k]
-            out = advance(x, lam_ref[first + t, above], lam_ref[first + t, below], coeffs)
+            out = advance(lam_ref[t, k], lam_ref[t, above], lam_ref[t, below], coeffs)
             out += jnp.where(row == lons - 1, halo[0, t, pl.ds(k, 1), :], 0.0)
             out += jnp.where(row == 0, halo[1, t, pl.ds(k, 1), :], 0.0)
-            out_ref[t, k] = out
-        return 0
-
-    lax.fori_loop(0, levels, level, 0)
-    for t in range(tracers):
-        out_ref[t, levels - 1] += rows_ref[first + t].astype(F32)
+            out_ref[t, n] = out
+        return 0
+
+    lax.fori_loop(0, held, level, 0)
+
+    @pl.when(step == levels // held - 1)
+    def _():
+        for t in range(tracers):
+            out_ref[t, held - 1] += rows_ref[t].astype(F32)
 
 
 def per_device(tiles, ranks, adjoint_state, met_fields, forcing, cluster_ids, hour_index):
@@ -355,7 +362,7 @@
             pltpu.VMEM((2, levels, lats), BF16),
             pltpu.VMEM(both, BF16),
             pltpu.VMEM((10, levels, lats), F32),
-            pltpu.SemaphoreType.DMA((5,)),
+            pltpu.SemaphoreType.DMA((8,)),
             pltpu.SemaphoreType.DMA((STEPS, ranks)),
             pltpu.SemaphoreType.DMA((STEPS, ranks)),
             pltpu.SemaphoreType.DMA((3, 2)),
@@ -367,15 +374,14 @@
         name="first_step",
     )(*arrays)
 
-    block = 4 if tracers % 4 == 0 else 1
-    state = pl.BlockSpec((block, levels, lons, lats), lambda t: (t, 0, 0, 0))
+    held = 4 if levels % 4 == 0 else 1
     return pl.pallas_call(
         second_step,
-        grid=(tracers // block,),
+        grid=(levels // held,),
         out_shape=jax.ShapeDtypeStruct(adjoint_state.shape, F32),
         in_specs=[vmem] * 4,
-        out_specs=state,
-        scratch_shapes=[pltpu.VMEM((2, block, levels, lats), F32)],
+        out_specs=pl.BlockSpec((tracers, held, lons, lats), lambda k: (0, k, 0, 0)),
+        scratch_shapes=[pltpu.VMEM(both, F32)],
         compiler_params=pltpu.CompilerParams(vmem_limit_bytes=40 << 20),
         name="second_step",
     )(lam1, met1, halo, rows)

time: 36.4 us -> 27.7 us (0.76)
  Pallas kernels: 36.2 us -> 27.5 us
    pallas_call x1, Pallas kernels: 27.3 us -> 22.5 us  [per_device(): pl.pallas_call(functools.partial(first_step, tiles, ranks), out_shape=(ja...]
    pallas_call x1, Pallas kernels: 8.88 us -> 5.03 us  [per_device(): pl.pallas_call(second_step, grid=(levels // held,), out_shape=jax.ShapeDt...]
where the time goes in v3:
time: 27.7 us; the launch traced here: 27.5 us
  Pallas kernels  27.5 us (99%)
    pallas_call x1, Pallas kernels, per_device(): pl.pallas_call(functools.partial(first_step, tiles, ranks), out_shape=(ja...  22.5 us
    pallas_call x1, Pallas kernels, per_device(): pl.pallas_call(second_step, grid=(levels // held,), out_shape=jax.ShapeDt...  5.03 us

profile of v3, /device:TPU:0, one launch (start us, length us, event | category | flops | bytes accessed | tf_op | source)
XLA Modules:
  0.0 27.5 jit_solution(8050318941209864503)
XLA Ops:
  0.0 22.5 %first_step.1 = (f32[16,16,16,256]{3,2,1,0:T(8,128)S(1)}, bf16[3,16,16,256]{3,2,1,0:T(8,128)(2,1)S(1)}, bf16[2,16,16,256]{3,2,1,0:T(8,128)(2,1)S(1)}, bf16[16,16,256]{2,1,0:T(8,128)(2,1)S(1)}) custom-call(s32[2]{0:T(128)} %hour_hbm.1, s32[16]{0:T(128)} %ids_hbm.1, f32[16,16,16,256]{3,2,1,0:T(8,128)} %lam_hbm.1, bf16[12,3,4,16,256]{4,3,2,1,0:T(8,128)(2,1)} %met_hbm.1, ...), custom_call_target="tpu_custom_call" | custom-call | tf_op jit(solution)/shard_map/first_step/pallas_call | solution.py:341
  22.5 5.0 %second_step.1 = f32[16,16,16,256]{3,2,1,0:T(8,128)} custom-call(f32[16,16,16,256]{3,2,1,0:T(8,128)S(1)} %get-tuple-element.9.lam_ref, bf16[3,16,16,256]{3,2,1,0:T(8,128)(2,1)S(1)} %get-tuple-element.10.met_ref, bf16[2,16,16,256]{3,2,1,0:T(8,128)(2,1)S(1)} %get-tuple-element.11.halo_ref, bf16[16,16,256]{2,1,0:T(8,128)(2,1)S(1)} %get-tuple-element.12.rows_ref), custom_call_target="tpu_custom_call" | custom-call | tf_op jit(solution)/shard_map/second_step/pallas_call | solution.py:378

commit v4 on v3

--- a/solution.py
+++ b/solution.py
@@ -50,7 +50,7 @@
     return out
 
 
-def first_step(
+def both_steps(
     tiles,
     ranks,
     hour_hbm,
@@ -58,13 +58,14 @@
     lam_hbm,
     met_hbm,
     forcing_hbm,
-    lam1,
+    lam2,
+    halo_ref,
     met1_ref,
-    halo_ref,
     rows_ref,
     hour_ref,
     ids_ref,
     lam,
+    lam1,
     met_ref,
     forcing_ref,
     met0,
@@ -80,6 +81,8 @@
     grecv,
     hsend,
     hrecv,
+    fsend,
+    frecv,
 ):
     tracers, levels, lons, _ = lam.shape
     share = levels // ranks
@@ -214,28 +217,32 @@
     for c in cx_copies:
         c.start()
 
-    def level(k, _):
-        coeffs = level_coeffs(lambda f, n: met0[f, n], k, levels)
-        above = jnp.minimum(k + 1, levels - 1)
-        below = jnp.maximum(k - 1, 0)
-
+    def run_levels(first, end, new, old, met):
+        def level(k, _):
+            coeffs = level_coeffs(lambda f, n: met[f, n], k, levels)
+            above = jnp.minimum(k + 1, levels - 1)
+            below = jnp.maximum(k - 1, 0)
+
+            def one(t, _):
+                new[t, k] = advance(old[t, k], old[t, above], old[t, below], coeffs)
+                return 0
+
+            lax.fori_loop(0, tracers, one, 0, unroll=True)
+            return 0
+
+        lax.fori_loop(first, end, level, 0)
+
+    def add_rows(new):
         def one(t, _):
-            lam1[t, k] = advance(lam[t, k], lam[t, above], lam[t, below], coeffs)
+            new[t, levels - 1] += rows_ref[t].astype(F32)
             return 0
 
         lax.fori_loop(0, tracers, one, 0, unroll=True)
-        return 0
-
-    lax.fori_loop(0, levels // 2, level, 0)
+
+    run_levels(0, levels // 2, lam1, lam, met0)
     forward(1, passed_on)
-    lax.fori_loop(levels // 2, levels, level, 0)
-
-    def add_rows(t, _):
-        lam1[t, levels - 1] += rows_ref[t].astype(F32)
-        return 0
-
-    lax.fori_loop(0, tracers, add_rows, 0, unroll=True)
-
+    run_levels(levels // 2, levels, lam1, lam, met0)
+    add_rows(lam1)
     forward(1, kept)
 
     def pick_next(k, _):
@@ -268,6 +275,19 @@
         centre = 1.0 - jnp.abs(cx) - jnp.abs(cy) - up - down
         return centre, up, down, from_east, from_west, north, south, leaves
 
+    def flux_copy(side, part):
+        cut = pl.ds(part * half, half)
+        return pltpu.make_async_remote_copy(
+            src_ref=flux_out.at[side, cut],
+            dst_ref=halo_ref.at[side, cut],
+            send_sem=fsend.at[side, part],
+            recv_sem=frecv.at[side, part],
+            device_id=((west, east)[side], rank),
+            device_id_type=MESH,
+        )
+
+    halves = 2 if tracers % 2 == 0 else 1
+    half = tracers // halves
     flux_copies = []
     for side in (0, 1):
         centre, up, down, from_east, from_west, north, south, leaves = edge_coeffs(side)
@@ -288,10 +308,14 @@
             lam1[t, :, c, :] = out
             return 0
 
-        lax.fori_loop(0, tracers, edge, 0, unroll=True)
-        copy = halo_copy(2, flux_out, halo_ref, side)
-        copy.start()
-        flux_copies.append(copy)
+        for part in range(halves):
+            lax.fori_loop(part * half, (part + 1) * half, edge, 0, unroll=True)
+            copy = flux_copy(side, part)
+            copy.start()
+            flux_copies.append(copy)
+
+    run_levels(0, levels, lam2, lam1, met1_ref)
+    add_rows(lam2)
 
     for copy in gathers.values():
         copy.wait_send()
@@ -299,7 +323,7 @@
         copy.wait()
 
 
-def second_step(lam_ref, met_ref, halo_ref, rows_ref, out_ref, halo):
+def add_halo(lam_ref, halo_ref, out_ref, halo):
     tracers, levels, lons, _ = lam_ref.shape
     held = out_ref.shape[1]
     step = pl.program_id(0)
@@ -312,22 +336,14 @@
 
     def level(n, _):
         k = step * held + n
-        coeffs = level_coeffs(lambda f, m: met_ref[f, m], k, levels)
-        above = jnp.minimum(k + 1, levels - 1)
-        below = jnp.maximum(k - 1, 0)
         for t in range(tracers):
-            out = advance(lam_ref[t, k], lam_ref[t, above], lam_ref[t, below], coeffs)
+            out = lam_ref[t, k]
             out += jnp.where(row == lons - 1, halo[0, t, pl.ds(k, 1), :], 0.0)
             out += jnp.where(row == 0, halo[1, t, pl.ds(k, 1), :], 0.0)
             out_ref[t, n] = out
         return 0
 
     lax.fori_loop(0, held, level, 0)
-
-    @pl.when(step == levels // held - 1)
-    def _():
-        for t in range(tracers):
-            out_ref[t, held - 1] += rows_ref[t].astype(F32)
 
 
 def per_device(tiles, ranks, adjoint_state, met_fields, forcing, cluster_ids, hour_index):
@@ -338,19 +354,20 @@
     both = (2, tracers, levels, lats)
     arrays = (hour_index, cluster_ids, adjoint_state, met_fields, forcing)
     arrays = [pltpu.with_memory_space_constraint(x, pltpu.HBM) for x in arrays]
-    lam1, met1, halo, rows = pl.pallas_call(
-        functools.partial(first_step, tiles, ranks),
+    lam2, halo = pl.pallas_call(
+        functools.partial(both_steps, tiles, ranks),
         out_shape=(
             jax.ShapeDtypeStruct(adjoint_state.shape, F32),
-            jax.ShapeDtypeStruct((fields, levels, lons, lats), BF16),
             jax.ShapeDtypeStruct(both, BF16),
-            jax.ShapeDtypeStruct((tracers, lons, lats), BF16),
         ),
         in_specs=[hbm] * 5,
-        out_specs=(vmem,) * 4,
+        out_specs=(vmem,) * 2,
         scratch_shapes=[
+            pltpu.VMEM((fields, levels, lons, lats), BF16),
+            pltpu.VMEM((tracers, lons, lats), BF16),
             pltpu.SMEM(hour_index.shape, jnp.int32),
             pltpu.SMEM(cluster_ids.shape, jnp.int32),
+            pltpu.VMEM(adjoint_state.shape, F32),
             pltpu.VMEM(adjoint_state.shape, F32),
             pltpu.VMEM(met_fields.shape, BF16),
             pltpu.VMEM(forcing.shape, BF16),
@@ -365,26 +382,28 @@
             pltpu.SemaphoreType.DMA((8,)),
             pltpu.SemaphoreType.DMA((STEPS, ranks)),
             pltpu.SemaphoreType.DMA((STEPS, ranks)),
-            pltpu.SemaphoreType.DMA((3, 2)),
-            pltpu.SemaphoreType.DMA((3, 2)),
+            pltpu.SemaphoreType.DMA((2, 2)),
+            pltpu.SemaphoreType.DMA((2, 2)),
+            pltpu.SemaphoreType.DMA((2, 2)),
+            pltpu.SemaphoreType.DMA((2, 2)),
         ],
         compiler_params=pltpu.CompilerParams(
             collective_id=0, has_side_effects=True, vmem_limit_bytes=40 << 20
         ),
-        name="first_step",
+        name="both_steps",
     )(*arrays)
 
     held = 4 if levels % 4 == 0 else 1
     return pl.pallas_call(
-        second_step,
+        add_halo,
         grid=(levels // held,),
         out_shape=jax.ShapeDtypeStruct(adjoint_state.shape, F32),
-        in_specs=[vmem] * 4,
+        in_specs=[vmem] * 2,
         out_specs=pl.BlockSpec((tracers, held, lons, lats), lambda k: (0, k, 0, 0)),
         scratch_shapes=[pltpu.VMEM(both, F32)],
         compiler_params=pltpu.CompilerParams(vmem_limit_bytes=40 << 20),
-        name="second_step",
-    )(lam1, met1, halo, rows)
+        name="add_halo",
+    )(lam2, halo)
 
 
 def solution(mesh):

time: 27.7 us -> 25.2 us (0.910)
  Pallas kernels: 27.5 us -> 25.1 us
    pallas_call x2, Pallas kernels: 27.5 us -> 25.1 us  [the longest x1 22.4 us: per_device(): pl.pallas_call(functools.partial(both_steps, tiles, ranks), out_shape=(ja...]
where the time goes in v4:
time: 25.2 us; the launch traced here: 25.1 us
  Pallas kernels  25.1 us (100%)
    pallas_call x1, Pallas kernels, per_device(): pl.pallas_call(functools.partial(both_steps, tiles, ranks), out_shape=(ja...  22.4 us
    pallas_call x1, Pallas kernels, per_device(): pl.pallas_call(add_halo, grid=(levels // held,), out_shape=jax.ShapeDtype...  2.66 us

profile of v4, /device:TPU:0, one launch (start us, length us, event | category | flops | bytes accessed | tf_op | source)
XLA Modules:
  0.0 25.1 jit_solution(1391972384531851811)
XLA Ops:
  0.0 22.4 %both_steps.1 = (f32[16,16,16,256]{3,2,1,0:T(8,128)S(1)}, bf16[2,16,16,256]{3,2,1,0:T(8,128)(2,1)S(1)}) custom-call(s32[2]{0:T(128)} %hour_hbm.1, s32[16]{0:T(128)} %ids_hbm.1, f32[16,16,16,256]{3,2,1,0:T(8,128)} %lam_hbm.1, bf16[12,3,4,16,256]{4,3,2,1,0:T(8,128)(2,1)} %met_hbm.1, bf16[64,16,256]{2,1,0:T(8,128)(2,1)} %forcing_hbm.1), custom_call_target="tpu_custom_call" | custom-call | tf_op jit(solution)/shard_map/both_steps/pallas_call | solution.py:357
  22.4 2.7 %add_halo.1 = f32[16,16,16,256]{3,2,1,0:T(8,128)} custom-call(f32[16,16,16,256]{3,2,1,0:T(8,128)S(1)} %get-tuple-element.7.lam_ref, bf16[2,16,16,256]{3,2,1,0:T(8,128)(2,1)S(1)} %get-tuple-element.8.halo_ref), custom_call_target="tpu_custom_call" | custom-call | tf_op jit(solution)/shard_map/add_halo/pallas_call | solution.py:397

commit v5 on v4

--- a/solution.py
+++ b/solution.py
@@ -239,10 +239,9 @@
 
         lax.fori_loop(0, tracers, one, 0, unroll=True)
 
-    run_levels(0, levels // 2, lam1, lam, met0)
+    run_levels(0, levels // 4, lam1, lam, met0)
     forward(1, passed_on)
-    run_levels(levels // 2, levels, lam1, lam, met0)
-    add_rows(lam1)
+    run_levels(levels // 4, levels // 2, lam1, lam, met0)
     forward(1, kept)
 
     def pick_next(k, _):
@@ -305,7 +304,7 @@
             out += shifted(x, 1, 1) * north + shifted(x, -1, 1) * south
             out += jnp.where(top, rows_ref[t].astype(F32)[c : c + 1], 0.0)
             flux_out[side, t] = (out * leaves).astype(BF16)
-            lam1[t, :, c, :] = out
+            edges[(0, 3)[side], t] = out
             return 0
 
         for part in range(halves):
@@ -313,6 +312,16 @@
             copy = flux_copy(side, part)
             copy.start()
             flux_copies.append(copy)
+
+    run_levels(levels // 2, levels, lam1, lam, met0)
+    add_rows(lam1)
+
+    def put(t, _):
+        lam1[t, :, 0, :] = edges[0, t]
+        lam1[t, :, last, :] = edges[3, t]
+        return 0
+
+    lax.fori_loop(0, tracers, put, 0, unroll=True)
 
     run_levels(0, levels, lam2, lam1, met1_ref)
     add_rows(lam2)

time: 25.2 us -> 24.6 us (0.976)
  Pallas kernels: 25.1 us -> 24.5 us
    pallas_call x1, Pallas kernels: 22.4 us -> 21.8 us  [per_device(): pl.pallas_call(functools.partial(both_steps, tiles, ranks), out_shape=(ja...]
where the time goes in v5:
time: 24.6 us; the launch traced here: 24.5 us
  Pallas kernels  24.5 us (100%)
    pallas_call x1, Pallas kernels, per_device(): pl.pallas_call(functools.partial(both_steps, tiles, ranks), out_shape=(ja...  21.8 us
    pallas_call x1, Pallas kernels, per_device(): pl.pallas_call(add_halo, grid=(levels // held,), out_shape=jax.ShapeDtype...  2.66 us

profile of v5, /device:TPU:0, one launch (start us, length us, event | category | flops | bytes accessed | tf_op | source)
XLA Modules:
  0.0 24.5 jit_solution(98148648716144284)
XLA Ops:
  0.0 21.8 %both_steps.1 = (f32[16,16,16,256]{3,2,1,0:T(8,128)S(1)}, bf16[2,16,16,256]{3,2,1,0:T(8,128)(2,1)S(1)}) custom-call(s32[2]{0:T(128)} %hour_hbm.1, s32[16]{0:T(128)} %ids_hbm.1, f32[16,16,16,256]{3,2,1,0:T(8,128)} %lam_hbm.1, bf16[12,3,4,16,256]{4,3,2,1,0:T(8,128)(2,1)} %met_hbm.1, bf16[64,16,256]{2,1,0:T(8,128)(2,1)} %forcing_hbm.1), custom_call_target="tpu_custom_call" | custom-call | tf_op jit(solution)/shard_map/both_steps/pallas_call | solution.py:366
  21.8 2.7 %add_halo.1 = f32[16,16,16,256]{3,2,1,0:T(8,128)} custom-call(f32[16,16,16,256]{3,2,1,0:T(8,128)S(1)} %get-tuple-element.7.lam_ref, bf16[2,16,16,256]{3,2,1,0:T(8,128)(2,1)S(1)} %get-tuple-element.8.halo_ref), custom_call_target="tpu_custom_call" | custom-call | tf_op jit(solution)/shard_map/add_halo/pallas_call | solution.py:406

commit v6 on v5

--- a/solution.py
+++ b/solution.py
@@ -83,6 +83,8 @@
     hrecv,
     fsend,
     frecv,
+    lsend,
+    lrecv,
 ):
     tracers, levels, lons, _ = lam.shape
     share = levels // ranks
@@ -170,9 +172,25 @@
         lam_out[1, t] = edges[3, t].astype(BF16)
         return 0
 
+    def lam_copy(side, part):
+        cut = pl.ds(part * some, some)
+        return pltpu.make_async_remote_copy(
+            src_ref=lam_out.at[side, cut],
+            dst_ref=lam_in.at[side, cut],
+            send_sem=lsend.at[side, part],
+            recv_sem=lrecv.at[side, part],
+            device_id=((west, east)[side], rank),
+            device_id_type=MESH,
+        )
+
+    lam_copies = []
     for n in range(parts):
         loads[3 + n].wait()
         lax.fori_loop(n * some, (n + 1) * some, pick, 0, unroll=True)
+        for side in (0, 1):
+            copy = lam_copy(side, n)
+            copy.start()
+            lam_copies.append(copy)
 
     def halo_copy(n, src, dst, side):
         return pltpu.make_async_remote_copy(
@@ -183,10 +201,6 @@
             device_id=((west, east)[side], rank),
             device_id_type=MESH,
         )
-
-    lam_copies = [halo_copy(0, lam_out, lam_in, side) for side in (0, 1)]
-    for c in lam_copies:
-        c.start()
 
     loads[2].wait()
     loads[-1].wait()
@@ -395,6 +409,8 @@
             pltpu.SemaphoreType.DMA((2, 2)),
             pltpu.SemaphoreType.DMA((2, 2)),
             pltpu.SemaphoreType.DMA((2, 2)),
+            pltpu.SemaphoreType.DMA((2, 4)),
+            pltpu.SemaphoreType.DMA((2, 4)),
         ],
         compiler_params=pltpu.CompilerParams(
             collective_id=0, has_side_effects=True, vmem_limit_bytes=40 << 20

time: 24.6 us -> 24.8 us (level)
  no operation moved by 1% of the time
where the time goes in v6:
time: 24.8 us; the launch traced here: 24.6 us
  Pallas kernels  24.6 us (99%)
    pallas_call x1, Pallas kernels, per_device(): pl.pallas_call(functools.partial(both_steps, tiles, ranks), out_shape=(ja...  22 us
    pallas_call x1, Pallas kernels, per_device(): pl.pallas_call(add_halo, grid=(levels // held,), out_shape=jax.ShapeDtype...  2.66 us

profile of v6, /device:TPU:0, one launch (start us, length us, event | category | flops | bytes accessed | tf_op | source)
XLA Modules:
  0.0 24.6 jit_solution(996273066375434864)
XLA Ops:
  0.0 22.0 %both_steps.1 = (f32[16,16,16,256]{3,2,1,0:T(8,128)S(1)}, bf16[2,16,16,256]{3,2,1,0:T(8,128)(2,1)S(1)}) custom-call(s32[2]{0:T(128)} %hour_hbm.1, s32[16]{0:T(128)} %ids_hbm.1, f32[16,16,16,256]{3,2,1,0:T(8,128)} %lam_hbm.1, bf16[12,3,4,16,256]{4,3,2,1,0:T(8,128)(2,1)} %met_hbm.1, bf16[64,16,256]{2,1,0:T(8,128)(2,1)} %forcing_hbm.1), custom_call_target="tpu_custom_call" | custom-call | tf_op jit(solution)/shard_map/both_steps/pallas_call | solution.py:380
  22.0 2.7 %add_halo.1 = f32[16,16,16,256]{3,2,1,0:T(8,128)} custom-call(f32[16,16,16,256]{3,2,1,0:T(8,128)S(1)} %get-tuple-element.7.lam_ref, bf16[2,16,16,256]{3,2,1,0:T(8,128)(2,1)S(1)} %get-tuple-element.8.halo_ref), custom_call_target="tpu_custom_call" | custom-call | tf_op jit(solution)/shard_map/add_halo/pallas_call | solution.py:422
